TPU v7x, 32 devices: a whole 2x2x4 slice. The times are simulated.
32 devices in a mesh: dom: 4 (over x, core), band: 8 (over z, y).
Axes of the slice: x: 2, y: 2, z: 4, core: 2. Of those that a mesh axis runs over, the one named last changes fastest.
Arguments:
- orbitals: bfloat16 [1024, 4, 2, 16, 128], P('band', 'dom'), may hold values from -6 to 6
- potential: float32 [4, 2, 16, 128], P('dom'), may hold values from -1 to 1
- ritz: bfloat16 [1024, 1024], P(None, 'band'), may hold values from -0.1875 to 0.1875
Outputs:
- rotated: float32 [1024, 4, 2, 16, 128], P('band', 'dom')
All inputs are finite; a program needn't handle non-finite values.
Results may differ from a plain program's by a relative error of at most 0.0029.
Values may be sent and summed in bfloat16 or wider, within the bound.
A program may use at most 64 MiB of HBM per device.

v0:
```python
import math

import jax
import jax.numpy as jnp
from jax import lax
from jax.sharding import PartitionSpec as P

DEG = 4


lower_bound = -1.5
cut_off = 1.0
upper_bound = 9.5
coef_zero = -2.5
coef_one = 4.0 / 3.0
coef_two = -1.0 / 12.0


def shifted(value, axis, steps):
    count = lax.axis_size(axis)
    pairs = [(source, (source + steps) % count) for source in range(count)]
    return lax.ppermute(value, axis, pairs)


def filter_weights(degree):
    half_width = (upper_bound - cut_off) / 2.0
    centre = (upper_bound + cut_off) / 2.0
    sigma_now = half_width / (lower_bound - centre)
    first_scale = sigma_now / half_width
    inverse_gain = 2.0 / sigma_now
    weights = []
    for degree_step in range(1, degree):
        sigma_next = 1.0 / (inverse_gain - sigma_now)
        weights.append((2.0 * sigma_next / half_width, sigma_now * sigma_next))
        sigma_now = sigma_next
    return (centre, first_scale, weights)


def send_first(face, offset):
    return shifted(face, "dom", offset)


def send_second(face, offset):
    return shifted(face, "dom", offset)


def padded_second(padded, count, axis):
    lower_near = lax.slice_in_dim(padded, 1, count + 1, axis=axis)
    upper_near = lax.slice_in_dim(padded, 3, count + 3, axis=axis)
    lower_far = lax.slice_in_dim(padded, 0, count, axis=axis)
    upper_far = lax.slice_in_dim(padded, 4, count + 4, axis=axis)
    return coef_one * (lower_near + upper_near) + coef_two * (lower_far + upper_far)


def apply_ham(field_now, local_pot, grid_side, row_y):
    cells_x = field_now.shape[1]
    cells_y = field_now.shape[2]
    low_x = send_first(field_now, grid_side)
    high_x = send_first(field_now, -grid_side)
    along_x = jnp.concatenate([low_x, field_now, high_x], axis=1)
    top_y = field_now[:, :, cells_y - 2 :]
    bottom_y = field_now[:, :, :2]
    low_y = jnp.where(row_y == 0, send_second(top_y, 1 - grid_side), send_second(top_y, 1))
    high_y = jnp.where(
        row_y == grid_side - 1, send_second(bottom_y, grid_side - 1), send_second(bottom_y, -1)
    )
    along_y = jnp.concatenate([low_y, field_now, high_y], axis=2)
    near_z = jnp.roll(field_now, 1, 3) + jnp.roll(field_now, -1, 3)
    far_z = jnp.roll(field_now, 2, 3) + jnp.roll(field_now, -2, 3)
    second = (
        3.0 * coef_zero * field_now
        + padded_second(along_x, cells_x, 1)
        + padded_second(along_y, cells_y, 2)
    )
    second = second + (coef_one * near_z + coef_two * far_z)
    return -0.5 * second + local_pot * field_now


def on_device(orbitals, potential, ritz):
    grid_side = math.isqrt(lax.axis_size("dom"))
    row_y = lax.axis_index("dom") % grid_side
    centre, first_scale, weights = filter_weights(DEG)
    local_pot = potential[0]
    previous = orbitals[:, 0].astype(jnp.float32)
    current = (apply_ham(previous, local_pot, grid_side, row_y) - centre * previous) * first_scale
    for scale_h, scale_x in weights:
        following = (
            apply_ham(current, local_pot, grid_side, row_y) - centre * current
        ) * scale_h - scale_x * previous
        previous, current = (current, following)
    band_rows = current.shape[0]
    flat_panel = current.astype(jnp.bfloat16).reshape(band_rows, -1)
    full_ritz = lax.all_gather(ritz, "band", axis=1, tiled=True)
    band_groups = lax.axis_size("band")
    sectioned = flat_panel.reshape(band_rows, band_groups, 1, -1)
    block = lax.all_to_all(sectioned, "band", split_axis=1, concat_axis=0, tiled=True)
    all_bands = block.shape[0]
    item_count = block.shape[2]
    lane_count = block.shape[3]
    mixed = lax.dot_general(
        full_ritz,
        block.reshape(all_bands, -1),
        (((0,), (0,)), ((), ())),
        preferred_element_type=jnp.float32,
    )
    mixed = mixed.reshape(all_bands, 1, item_count, lane_count)
    returned = lax.all_to_all(mixed, "band", split_axis=0, concat_axis=1, tiled=True)
    rotated = returned.reshape(band_rows, -1)
    return rotated.reshape(orbitals.shape)


def solution(mesh):
    in_specs = (P("band", "dom", None, None, None), P("dom", None, None, None), P(None, "band"))
    out_specs = P("band", "dom", None, None, None)
    return jax.shard_map(
        on_device, mesh=mesh, in_specs=in_specs, out_specs=out_specs, check_vma=False
    )
```

profile of v0, /device:TPU:0, one launch (start us, length us, event | category | flops | bytes accessed | tf_op | source)
XLA Modules:
  0.0 373.4 jit_solution(4609436577403534129)
XLA Ops:
  6.5 1.9 copy.9
  8.7 3.0 collective-permute-start
  12.5 1.7 collective-permute-start.4
  14.7 2.4 fusion.101
  17.2 2.4 fusion.103
  19.6 42.6 %collective-permute-done.3 = f32[128,2,2,128]{0,3,2,1:T(8,128)} collective-permute-done((f32[128,2,2,128]{0,3,2,1:T(8,128)}, f32[128,2,2,128]{0,3,2,1:T(8,128)}, u32[]{:S(2)}, u32[]{:S(2)}) %collective-permute-start.3) | collective-permute-done | bytes 262176 | tf_op jit(solution)/shard_map/ppermute | solution.py:22
  62.3 1.2 collective-permute-done.4
  64.5 3.4 collective-permute-done.1
  68.9 6.6 %broadcast_multiply_fusion = (f32[128,2,16,128]{0,3,2,1:T(8,128)S(1)}, f32[128,2,16,128]{0,3,2,1:T(8,128)S(1)}) fusion(f32[2,16,128]{2,1,0:T(8,128)S(1)} %bitcast.32, f32[128,2,16,2]{0,3,2,1:T(2,128)S(1)} %get-tuple-element.44, f32[128,2,16,126]{0,3,2,1:T(8,128)} %get-tuple-element.46, f32[128,2,16,126]{0,3,2,1:T(8,128)} %get-tuple-element.45, ...), kind=kLoop, calls=%fused_computation.129 | loop fusion | flops 18874368 | bytes 18366464 | tf_op jit(solution)/shard_map/mul | solution.py:85
  75.5 1.5 collective-permute-start.5
  77.9 1.7 collective-permute-start.8
  80.7 47.9 %collective-permute-done.6 = f32[128,2,2,128]{0,3,2,1:T(8,128)S(1)} collective-permute-done((f32[128,2,2,128]{0,3,2,1:T(8,128)S(1)}, f32[128,2,2,128]{0,3,2,1:T(8,128)S(1)}, u32[]{:S(2)}, u32[]{:S(2)}) %collective-permute-start.6) | collective-permute-done | bytes 262176 | tf_op jit(solution)/shard_map/ppermute | solution.py:22
  129.1 5.6 %collective-permute-done.8 = f32[128,2,2,128]{0,3,2,1:T(8,128)S(1)} collective-permute-done((f32[128,2,2,128]{0,3,2,1:T(8,128)S(1)}, f32[128,2,2,128]{0,3,2,1:T(8,128)S(1)}, u32[]{:S(2)}, u32[]{:S(2)}) %collective-permute-start.8) | collective-permute-done | bytes 262176 | tf_op jit(solution)/shard_map/ppermute | solution.py:22
  134.8 5.9 %fusion.34 = f32[128,2,16,128]{0,3,2,1:T(8,128)S(1)} fusion(f32[128,2,16,128]{0,3,2,1:T(8,128)S(1)} %get-tuple-element.5, f32[128,2,2,128]{0,3,2,1:T(8,128)S(1)} %broadcast_select_fusion.2, f32[128,2,2,128]{0,3,2,1:T(8,128)S(1)} %broadcast_select_fusion.6, f32[128,2,16,128]{0,3,2,1:T(8,128)S(1)} %collective-permute-done.5, ...), kind=kLoop, calls=%fused_computation.50 | loop fusion | flops 19922944 | bytes 18366464 | tf_op jit(solution)/shard_map/sub | solution.py:87
  140.7 2.1 collective-permute-start.10
  146.1 48.3 %collective-permute-done.11 = f32[128,2,2,128]{0,3,2,1:T(8,128)S(1)} collective-permute-done((f32[128,2,2,128]{0,3,2,1:T(8,128)S(1)}, f32[128,2,2,128]{0,3,2,1:T(8,128)S(1)}, u32[]{:S(2)}, u32[]{:S(2)}) %collective-permute-start.11) | collective-permute-done | bytes 262176 | tf_op jit(solution)/shard_map/ppermute | solution.py:22
  194.4 4.9 %collective-permute-done.13 = f32[128,2,2,128]{0,3,2,1:T(8,128)S(1)} collective-permute-done((f32[128,2,2,128]{0,3,2,1:T(8,128)S(1)}, f32[128,2,2,128]{0,3,2,1:T(8,128)S(1)}, u32[]{:S(2)}, u32[]{:S(2)}) %collective-permute-start.13) | collective-permute-done | bytes 262176 | tf_op jit(solution)/shard_map/ppermute | solution.py:22
  199.4 6.5 %fusion.22 = f32[128,2,16,128]{0,3,2,1:T(8,128)} fusion(f32[128,2,16,128]{0,3,2,1:T(8,128)S(1)} %fusion.34, f32[128,2,2,128]{0,3,2,1:T(8,128)S(1)} %broadcast_select_fusion.1, f32[128,2,2,128]{0,3,2,1:T(8,128)S(1)} %broadcast_select_fusion.5, f32[128,2,16,128]{0,3,2,1:T(8,128)S(1)} %collective-permute-done.10, f32[128,2,16,127]{0,3,2,1:T(8,128)S(1)} %get-tuple-element.22, ...), kind=kLoop, calls=%fused_computation.38 | loop fusion | flops 19398656 | bytes 17317888 | tf_op jit(solution)/shard_map/sub | solution.py:87
  205.9 1.4 collective-permute-start.15
  207.4 1.1 fusion.84
  209.0 1.6 collective-permute-start.18
  210.8 2.7 fusion.86
  213.5 2.9 fusion.88
  218.4 40.8 %collective-permute-done.16 = f32[128,2,2,128]{0,3,2,1:T(8,128)S(1)} collective-permute-done((f32[128,2,2,128]{0,3,2,1:T(8,128)S(1)}, f32[128,2,2,128]{0,3,2,1:T(8,128)S(1)}, u32[]{:S(2)}, u32[]{:S(2)}) %collective-permute-start.16) | collective-permute-done | bytes 262176 | tf_op jit(solution)/shard_map/ppermute | solution.py:22
  259.2 5.5 %collective-permute-done.18 = f32[128,2,2,128]{0,3,2,1:T(8,128)S(1)} collective-permute-done((f32[128,2,2,128]{0,3,2,1:T(8,128)S(1)}, f32[128,2,2,128]{0,3,2,1:T(8,128)S(1)}, u32[]{:S(2)}, u32[]{:S(2)}) %collective-permute-start.18) | collective-permute-done | bytes 262176 | tf_op jit(solution)/shard_map/ppermute | solution.py:22
  264.7 8.4 %fusion.82 = bf16[128,2,16,128]{0,3,2,1:T(8,128)(2,1)S(1)} fusion(f32[128,2,16,128]{0,3,2,1:T(8,128)S(1)} %fusion.34, f32[128,2,16,128]{0,3,2,1:T(8,128)} %fusion.22, f32[128,2,16,2]{0,3,2,1:T(2,128)S(1)} %get-tuple-element.14, f32[128,2,16,126]{0,3,2,1:T(8,128)S(1)} %get-tuple-element.16, f32[128,2,16,126]{0,3,2,1:T(8,128)S(1)} %get-tuple-element.15, ...), kind=kLoop, calls=%fused_computation.126 | loop fusion | flops 19922944 | bytes 16269312 | tf_op jit(solution)/shard_map/convert_element_type | solution.py:92
  273.1 32.1 %all_to_all.30 = bf16[128,8,1,512]{0,3,2,1:T(8,128)(2,1)S(1)} all-to-all(bf16[128,8,1,512]{0,3,2,1:T(8,128)(2,1)S(1)} %bitcast.30), channel_id=1, replica_groups=mesh['dom'=4,'band'=8] {'band'}, dimensions={1} | all-to-all | bytes 2097152 | tf_op jit(solution)/shard_map/all_to_all | solution.py:96
  305.8 2.9 convolution_bitcast_fusion
  308.6 3.7 copy.12
  312.3 51.6 %all_to_all.31 = f32[1024,1,1,512]{3,2,1,0:T(1,128)S(1)} all-to-all(f32[1024,1,1,512]{3,2,1,0:T(1,128)} %copy.12), channel_id=1, replica_groups=mesh['dom'=4,'band'=8] {'band'}, dimensions={0} | all-to-all | bytes 4194304 | tf_op jit(solution)/shard_map/all_to_all | solution.py:107
  363.9 1.2 copy.13
  365.1 1.4 reshape_reshape.7
  (55 shorter events, 12.7 us)
Async XLA Ops:
  6.5 299.2 %all-gather.2.cloned.1.call-start = ((), (), s32[]{:S(2)}) async-start(), calls=%async_computation.2 | async-start | bytes 2359296 | tf_op jit(solution)/shard_map/all_gather | solution.py:93
  8.7 60.1 %collective-permute-start = (f32[128,2,16,128]{0,3,2,1:T(8,128)S(1)}, f32[128,2,16,128]{0,3,2,1:T(8,128)}, u32[]{:S(2)}, u32[]{:S(2)}) collective-permute-start(f32[128,2,16,128]{0,3,2,1:T(8,128)S(1)} %bitcast_convert_fusion), channel_id=1, source_target_pairs={{0,16},{8,24},{16,0},{24,8},{1,17},{9,25},{17,1},{25,9},{2,18},{10... | collective-permute-start | bytes 6291464 | tf_op jit(solution)/shard_map/ppermute | solution.py:22
  12.5 49.8 %collective-permute-start.3 = (f32[128,2,2,128]{0,3,2,1:T(8,128)}, f32[128,2,2,128]{0,3,2,1:T(8,128)}, u32[]{:S(2)}, u32[]{:S(2)}) collective-permute-start(f32[128,2,2,128]{0,3,2,1:T(8,128)} %get-tuple-element.38), channel_id=1, source_target_pairs={{0,8},{8,16},{16,24},{24,0},{1,9},{9,17},{17,25},{25,1},{2,10},{10... | collective-permute-start | bytes 786440 | tf_op jit(solution)/shard_map/ppermute | solution.py:22
  12.5 51.0 %collective-permute-start.4 = (f32[128,2,2,128]{0,3,2,1:T(8,128)}, f32[128,2,2,128]{0,3,2,1:T(8,128)}, u32[]{:S(2)}, u32[]{:S(2)}) collective-permute-start(f32[128,2,2,128]{0,3,2,1:T(8,128)} %get-tuple-element.38), channel_id=1, source_target_pairs={{0,24},{8,0},{16,8},{24,16},{1,25},{9,1},{17,9},{25,17},{2,26},{10... | collective-permute-start | bytes 786440 | tf_op jit(solution)/shard_map/ppermute | solution.py:22
  14.2 53.6 %collective-permute-start.1 = (f32[128,2,2,128]{0,3,2,1:T(8,128)S(1)}, f32[128,2,2,128]{0,3,2,1:T(8,128)}, u32[]{:S(2)}, u32[]{:S(2)}) collective-permute-start(f32[128,2,2,128]{0,3,2,1:T(8,128)S(1)} %get-tuple-element.37), channel_id=1, source_target_pairs={{0,24},{8,0},{16,8},{24,16},{1,25},{9,1},{17,9},{25,17},{2,26},{10... | collective-permute-start | bytes 786440 | tf_op jit(solution)/shard_map/ppermute | solution.py:22
  14.3 53.6 %collective-permute-start.2 = (f32[128,2,2,128]{0,3,2,1:T(8,128)S(1)}, f32[128,2,2,128]{0,3,2,1:T(8,128)}, u32[]{:S(2)}, u32[]{:S(2)}) collective-permute-start(f32[128,2,2,128]{0,3,2,1:T(8,128)S(1)} %get-tuple-element.37), channel_id=1, source_target_pairs={{0,8},{8,16},{16,24},{24,0},{1,9},{9,17},{17,25},{25,1},{2,10},{10... | collective-permute-start | bytes 786440 | tf_op jit(solution)/shard_map/ppermute | solution.py:22
  17.2 51.7 %copy-start = (f32[1,2,16,128]{3,2,1,0:T(8,128)S(1)}, f32[1,2,16,128]{3,2,1,0:T(8,128)}, u32[]{:S(2)}) copy-start(f32[1,2,16,128]{3,2,1,0:T(8,128)} %param.4) | copy-start | bytes 49156
  75.5 59.2 %collective-permute-start.5 = (f32[128,2,16,128]{0,3,2,1:T(8,128)S(1)}, f32[128,2,16,128]{0,3,2,1:T(8,128)S(1)}, u32[]{:S(2)}, u32[]{:S(2)}) collective-permute-start(f32[128,2,16,128]{0,3,2,1:T(8,128)S(1)} %get-tuple-element.5), channel_id=1, source_target_pairs={{0,16},{8,24},{16,0},{24,8},{1,17},{9,25},{17,1},{25,9},{2,18},{10... | collective-permute-start | bytes 6291464 | tf_op jit(solution)/shard_map/ppermute | solution.py:22
  77.1 51.6 %collective-permute-start.6 = (f32[128,2,2,128]{0,3,2,1:T(8,128)S(1)}, f32[128,2,2,128]{0,3,2,1:T(8,128)S(1)}, u32[]{:S(2)}, u32[]{:S(2)}) collective-permute-start(f32[128,2,2,128]{0,3,2,1:T(8,128)S(1)} %get-tuple-element.35), channel_id=1, source_target_pairs={{0,24},{8,0},{16,8},{24,16},{1,25},{9,1},{17,9},{25,17},{2,26},{10... | collective-permute-start | bytes 786440 | tf_op jit(solution)/shard_map/ppermute | solution.py:22
  77.7 51.4 %collective-permute-start.7 = (f32[128,2,2,128]{0,3,2,1:T(8,128)S(1)}, f32[128,2,2,128]{0,3,2,1:T(8,128)S(1)}, u32[]{:S(2)}, u32[]{:S(2)}) collective-permute-start(f32[128,2,2,128]{0,3,2,1:T(8,128)S(1)} %get-tuple-element.35), channel_id=1, source_target_pairs={{0,8},{8,16},{16,24},{24,0},{1,9},{9,17},{17,25},{25,1},{2,10},{10... | collective-permute-start | bytes 786440 | tf_op jit(solution)/shard_map/ppermute | solution.py:22
  77.9 56.8 %collective-permute-start.8 = (f32[128,2,2,128]{0,3,2,1:T(8,128)S(1)}, f32[128,2,2,128]{0,3,2,1:T(8,128)S(1)}, u32[]{:S(2)}, u32[]{:S(2)}) collective-permute-start(f32[128,2,2,128]{0,3,2,1:T(8,128)S(1)} %get-tuple-element.36), channel_id=1, source_target_pairs={{0,8},{8,16},{16,24},{24,0},{1,9},{9,17},{17,25},{25,1},{2,10},{10... | collective-permute-start | bytes 786440 | tf_op jit(solution)/shard_map/ppermute | solution.py:22
  79.5 55.2 %collective-permute-start.9 = (f32[128,2,2,128]{0,3,2,1:T(8,128)S(1)}, f32[128,2,2,128]{0,3,2,1:T(8,128)S(1)}, u32[]{:S(2)}, u32[]{:S(2)}) collective-permute-start(f32[128,2,2,128]{0,3,2,1:T(8,128)S(1)} %get-tuple-element.36), channel_id=1, source_target_pairs={{0,24},{8,0},{16,8},{24,16},{1,25},{9,1},{17,9},{25,17},{2,26},{10... | collective-permute-start | bytes 786440 | tf_op jit(solution)/shard_map/ppermute | solution.py:22
  140.7 58.7 %collective-permute-start.10 = (f32[128,2,16,128]{0,3,2,1:T(8,128)S(1)}, f32[128,2,16,128]{0,3,2,1:T(8,128)S(1)}, u32[]{:S(2)}, u32[]{:S(2)}) collective-permute-start(f32[128,2,16,128]{0,3,2,1:T(8,128)S(1)} %fusion.34), channel_id=1, source_target_pairs={{0,16},{8,24},{16,0},{24,8},{1,17},{9,25},{17,1},{25,9},{2,18},{10... | collective-permute-start | bytes 6291464 | tf_op jit(solution)/shard_map/ppermute | solution.py:22
  142.8 51.6 %collective-permute-start.11 = (f32[128,2,2,128]{0,3,2,1:T(8,128)S(1)}, f32[128,2,2,128]{0,3,2,1:T(8,128)S(1)}, u32[]{:S(2)}, u32[]{:S(2)}) collective-permute-start(f32[128,2,2,128]{0,3,2,1:T(8,128)S(1)} %get-tuple-element.25), channel_id=1, source_target_pairs={{0,24},{8,0},{16,8},{24,16},{1,25},{9,1},{17,9},{25,17},{2,26},{10... | collective-permute-start | bytes 786440 | tf_op jit(solution)/shard_map/ppermute | solution.py:22
  142.9 51.5 %collective-permute-start.12 = (f32[128,2,2,128]{0,3,2,1:T(8,128)S(1)}, f32[128,2,2,128]{0,3,2,1:T(8,128)S(1)}, u32[]{:S(2)}, u32[]{:S(2)}) collective-permute-start(f32[128,2,2,128]{0,3,2,1:T(8,128)S(1)} %get-tuple-element.25), channel_id=1, source_target_pairs={{0,8},{8,16},{16,24},{24,0},{1,9},{9,17},{17,25},{25,1},{2,10},{10... | collective-permute-start | bytes 786440 | tf_op jit(solution)/shard_map/ppermute | solution.py:22
  143.4 56.0 %collective-permute-start.13 = (f32[128,2,2,128]{0,3,2,1:T(8,128)S(1)}, f32[128,2,2,128]{0,3,2,1:T(8,128)S(1)}, u32[]{:S(2)}, u32[]{:S(2)}) collective-permute-start(f32[128,2,2,128]{0,3,2,1:T(8,128)S(1)} %get-tuple-element.26), channel_id=1, source_target_pairs={{0,8},{8,16},{16,24},{24,0},{1,9},{9,17},{17,25},{25,1},{2,10},{10... | collective-permute-start | bytes 786440 | tf_op jit(solution)/shard_map/ppermute | solution.py:22
  144.4 54.9 %collective-permute-start.14 = (f32[128,2,2,128]{0,3,2,1:T(8,128)S(1)}, f32[128,2,2,128]{0,3,2,1:T(8,128)S(1)}, u32[]{:S(2)}, u32[]{:S(2)}) collective-permute-start(f32[128,2,2,128]{0,3,2,1:T(8,128)S(1)} %get-tuple-element.26), channel_id=1, source_target_pairs={{0,24},{8,0},{16,8},{24,16},{1,25},{9,1},{17,9},{25,17},{2,26},{10... | collective-permute-start | bytes 786440 | tf_op jit(solution)/shard_map/ppermute | solution.py:22
  205.9 58.8 %collective-permute-start.15 = (f32[128,2,16,128]{0,3,2,1:T(8,128)}, f32[128,2,16,128]{0,3,2,1:T(8,128)}, u32[]{:S(2)}, u32[]{:S(2)}) collective-permute-start(f32[128,2,16,128]{0,3,2,1:T(8,128)} %fusion.22), channel_id=1, source_target_pairs={{0,16},{8,24},{16,0},{24,8},{1,17},{9,25},{17,1},{25,9},{2,18},{10... | collective-permute-start | bytes 6291464 | tf_op jit(solution)/shard_map/ppermute | solution.py:22
  208.4 50.7 %collective-permute-start.16 = (f32[128,2,2,128]{0,3,2,1:T(8,128)S(1)}, f32[128,2,2,128]{0,3,2,1:T(8,128)S(1)}, u32[]{:S(2)}, u32[]{:S(2)}) collective-permute-start(f32[128,2,2,128]{0,3,2,1:T(8,128)S(1)} %get-tuple-element.7), channel_id=1, source_target_pairs={{0,24},{8,0},{16,8},{24,16},{1,25},{9,1},{17,9},{25,17},{2,26},{10... | collective-permute-start | bytes 786440 | tf_op jit(solution)/shard_map/ppermute | solution.py:22
  208.8 50.4 %collective-permute-start.17 = (f32[128,2,2,128]{0,3,2,1:T(8,128)S(1)}, f32[128,2,2,128]{0,3,2,1:T(8,128)S(1)}, u32[]{:S(2)}, u32[]{:S(2)}) collective-permute-start(f32[128,2,2,128]{0,3,2,1:T(8,128)S(1)} %get-tuple-element.7), channel_id=1, source_target_pairs={{0,8},{8,16},{16,24},{24,0},{1,9},{9,17},{17,25},{25,1},{2,10},{10... | collective-permute-start | bytes 786440 | tf_op jit(solution)/shard_map/ppermute | solution.py:22
  209.0 55.7 %collective-permute-start.18 = (f32[128,2,2,128]{0,3,2,1:T(8,128)S(1)}, f32[128,2,2,128]{0,3,2,1:T(8,128)S(1)}, u32[]{:S(2)}, u32[]{:S(2)}) collective-permute-start(f32[128,2,2,128]{0,3,2,1:T(8,128)S(1)} %get-tuple-element.8), channel_id=1, source_target_pairs={{0,8},{8,16},{16,24},{24,0},{1,9},{9,17},{17,25},{25,1},{2,10},{10... | collective-permute-start | bytes 786440 | tf_op jit(solution)/shard_map/ppermute | solution.py:22
  210.6 54.1 %collective-permute-start.19 = (f32[128,2,2,128]{0,3,2,1:T(8,128)S(1)}, f32[128,2,2,128]{0,3,2,1:T(8,128)S(1)}, u32[]{:S(2)}, u32[]{:S(2)}) collective-permute-start(f32[128,2,2,128]{0,3,2,1:T(8,128)S(1)} %get-tuple-element.8), channel_id=1, source_target_pairs={{0,24},{8,0},{16,8},{24,16},{1,25},{9,1},{17,9},{25,17},{2,26},{10... | collective-permute-start | bytes 786440 | tf_op jit(solution)/shard_map/ppermute | solution.py:22
Sparse Core Ops, SparseCore 0:
  207.5 51.1 all-gather.1
where the time goes:
time: 374 us; the launch traced here: 373 us
  waiting for transfers between devices  201 us (54%)
  blocking collectives  83.7 us (22%)
  other arithmetic  29.8 us (8%)
  local copies, waits for them, and re-layouts  25.2 us (7%)
  starting transfers between devices  17.4 us (5%)
  between operations  13.7 us (4%)
    ppermute x20, waiting for transfers between devices, shifted(): return lax.ppermute(value, axis, pairs)  201 us
    all_to_all x1, blocking collectives, on_device(): lax.all_to_all(mixed, 'band', split_axis=0, concat_axis=1, tiled=True)  51.6 us
    all_to_all x1, blocking collectives, on_device(): lax.all_to_all(sectioned, 'band', split_axis=1, concat_axis=0, tiled=True)  32.1 us
    ppermute x20, starting transfers between devices, shifted(): return lax.ppermute(value, axis, pairs)  17.4 us
    sub x2, other arithmetic, on_device(): (apply_ham(current, local_pot, grid_side, row_y) - centre * current) * sc...  12.4 us
    convert_element_type x1, other arithmetic, on_device(): flat_panel = current.astype(jnp.bfloat16).reshape(band_rows, -1)  8.35 us
  transfers between devices with their start and end apart: 21, of which 10 were waited for; matrix products, arithmetic and copies ran while one was open for 7% of the time, Pallas kernels for 0%

commit v1 on v0

v1 whole, which is shorter than its diff:
```python
import functools
import math

import jax
import jax.numpy as jnp
from jax import lax
from jax.experimental import pallas as pl
from jax.experimental.pallas import tpu as pltpu
from jax.sharding import PartitionSpec as P

DEG = 4

lower_bound = -1.5
cut_off = 1.0
upper_bound = 9.5
coef_zero = -2.5
coef_one = 4.0 / 3.0
coef_two = -1.0 / 12.0


def filter_weights(degree):
    half_width = (upper_bound - cut_off) / 2.0
    centre = (upper_bound + cut_off) / 2.0
    sigma_now = half_width / (lower_bound - centre)
    first_scale = sigma_now / half_width
    inverse_gain = 2.0 / sigma_now
    weights = []
    for degree_step in range(1, degree):
        sigma_next = 1.0 / (inverse_gain - sigma_now)
        weights.append((2.0 * sigma_next / half_width, sigma_now * sigma_next))
        sigma_now = sigma_next
    return (centre, first_scale, weights)


def filter_kernel(side, cells_x, cells_y, in_ref, pot_ref, out_ref, even, odd):
    count_x, count_y = even.shape[0], even.shape[1]
    centre, first_scale, weights = filter_weights(DEG)
    diagonal = -0.5 * 3.0 * coef_zero - centre

    def block_of(x, y):
        dom = (x // cells_x) * side + y // cells_y
        row = (x % cells_x) * cells_y + y % cells_y
        return dom, row

    def load(y, x):
        dom, row = block_of(x, y)
        even[x, y] = in_ref[dom, row].astype(jnp.float32)

    for x in range(count_x):
        lax.fori_loop(0, count_y, lambda y, c, x=x: (load(y, x), c)[1], 0, unroll=4)

    def step(source, target, scale_h, scale_x, last):
        def row_step(y, x):
            at = lambda dx, dy: source[(x + dx) % count_x, lax.rem(y + dy + count_y, count_y)]
            here = source[x, y]
            near = (
                at(1, 0)
                + at(-1, 0)
                + (at(0, 1) + at(0, -1))
                + (pltpu.roll(here, 1, 1) + pltpu.roll(here, 127, 1))
            )
            far = (
                at(2, 0)
                + at(-2, 0)
                + (at(0, 2) + at(0, -2))
                + (pltpu.roll(here, 2, 1) + pltpu.roll(here, 126, 1))
            )
            dom, row = block_of(x, y)
            pot = pot_ref[dom, pl.ds(row, 1), :] + diagonal
            value = (pot * scale_h) * here + (
                (-0.5 * coef_one * scale_h) * near + (-0.5 * coef_two * scale_h) * far
            )
            if scale_x is not None:
                value = value - scale_x * target[x, y]
            if last:
                out_ref[dom, row] = value.astype(out_ref.dtype)
            else:
                target[x, y] = value

        for x in range(count_x):
            lax.fori_loop(0, count_y, lambda y, c, x=x: (row_step(y, x), c)[1], 0, unroll=4)

    step(even, odd, first_scale, None, False)
    source, target = odd, even
    for index, (scale_h, scale_x) in enumerate(weights):
        step(source, target, scale_h, scale_x, index == len(weights) - 1)
        source, target = target, source


def filter_bands(blocks, potential, side, cells_x, cells_y):
    doms, rows, bands, lanes = blocks.shape
    return pl.pallas_call(
        functools.partial(filter_kernel, side, cells_x, cells_y),
        out_shape=jax.ShapeDtypeStruct(blocks.shape, jnp.bfloat16),
        in_specs=[pl.BlockSpec(memory_space=pltpu.VMEM)] * 2,
        out_specs=pl.BlockSpec(memory_space=pltpu.VMEM),
        scratch_shapes=[
            pltpu.VMEM((side * cells_x, side * cells_y, bands, lanes), jnp.float32),
            pltpu.VMEM((side * cells_x, side * cells_y, bands, lanes), jnp.float32),
        ],
        compiler_params=pltpu.CompilerParams(vmem_limit_bytes=40 * 2**20),
        name="chebyshev",
    )(blocks, potential)


def on_device(orbitals, potential, ritz):
    doms = lax.axis_size("dom")
    groups = lax.axis_size("band")
    side = math.isqrt(doms)
    bands, _, cells_x, cells_y, lanes = orbitals.shape
    rows = cells_x * cells_y
    share = bands // doms
    full_ritz = lax.all_gather(ritz, "band", axis=1, tiled=True)
    full_pot = lax.all_gather(potential.reshape(1, rows, lanes), "dom", axis=0, tiled=True)
    panel = orbitals.reshape(bands, rows, lanes).transpose(1, 0, 2)
    panel = panel.reshape(rows, doms, share, lanes).transpose(1, 0, 2, 3)
    whole = lax.all_to_all(panel, "dom", split_axis=0, concat_axis=0, tiled=True)
    filtered = filter_bands(whole, full_pot, side, cells_x, cells_y)
    part = rows // groups
    pieces = filtered.reshape(doms, groups, part, share, lanes).transpose(1, 0, 2, 3, 4)
    pieces = pieces.reshape(groups * doms, part, share, lanes)
    block = lax.all_to_all(pieces, ("band", "dom"), split_axis=0, concat_axis=0, tiled=True)
    block = block.transpose(0, 2, 1, 3).reshape(groups * bands, part * lanes)
    mixed = lax.dot_general(
        full_ritz, block, (((0,), (0,)), ((), ())), preferred_element_type=jnp.float32
    )
    mixed = mixed.astype(jnp.bfloat16).reshape(groups, bands, part, lanes)
    returned = lax.all_to_all(mixed, "band", split_axis=0, concat_axis=0, tiled=True)
    rotated = returned.transpose(1, 0, 2, 3).reshape(bands, rows, lanes)
    return rotated.astype(jnp.float32).reshape(orbitals.shape)


def solution(mesh):
    in_specs = (P("band", "dom", None, None, None), P("dom", None, None, None), P(None, "band"))
    out_specs = P("band", "dom", None, None, None)
    return jax.shard_map(
        on_device, mesh=mesh, in_specs=in_specs, out_specs=out_specs, check_vma=False
    )
```

time: 374 us -> 127 us (0.34)
  waiting for transfers between devices: 201 us -> 0.73 us
  other arithmetic: 29.8 us -> 0.24 us
  local copies, waits for them, and re-layouts: 25.2 us -> 5.7 us
  Pallas kernels: 0 us -> 18.9 us
  starting transfers between devices: 17.4 us -> 4.23 us
    ppermute x20 -> x0, waiting for transfers between devices: 201 us -> none  [shifted(): return lax.ppermute(value, axis, pairs)]
    pallas_call x0 -> x1, Pallas kernels: none -> 18.9 us  [filter_bands(): pl.pallas_call(functools.partial(filter_kernel, side, cells_x, cells_y),...]
    all_to_all x2, blocking collectives: 83.7 us -> 65.1 us  [the longest x1 36.4 us: on_device(): lax.all_to_all(pieces, ('band', 'dom'), split_axis=0, concat_axis=0, tile...]
    ppermute x20 -> x0, starting transfers between devices: 17.4 us -> none  [shifted(): return lax.ppermute(value, axis, pairs)]
    slice x20 -> x0, local copies, waits for them, and re-layouts: 16.4 us -> none  [the longest x8 7.33 us: apply_ham(): far_z = jnp.roll(field_now, 2, 3) + jnp.roll(field_now, -2, 3)]
    all_gather x0 -> x1, blocking collectives: none -> 15.6 us  [on_device(): lax.all_gather(potential.reshape(1, rows, lanes), 'dom', axis=0, tiled=True)]
    sub x2 -> x0, other arithmetic: 12.4 us -> none  [on_device(): (apply_ham(current, local_pot, grid_side, row_y) - centre * current) * sc...]
    convert_element_type x2 -> x1, other arithmetic: 8.59 us -> 0.24 us  [on_device(): return rotated.astype(jnp.float32).reshape(orbitals.shape)]
  transfers between devices with their start and end apart: 21 -> 2, of which waited for: 10 -> 0; matrix products, arithmetic and copies ran while one was open for 7% -> 3% of each run, Pallas kernels for 0% -> 15%
where the time goes in v1:
time: 127 us
  blocking collectives  80.7 us (64%)
  Pallas kernels  18.9 us (15%)
  between operations  13.5 us (11%)
  local copies, waits for them, and re-layouts  5.7 us (4%)
  starting transfers between devices  4.23 us (3%)
  matrix products  2.86 us (2%)
    all_to_all x1, blocking collectives, on_device(): lax.all_to_all(pieces, ('band', 'dom'), split_axis=0, concat_axis=0, tile...  36.4 us
    all_to_all x1, blocking collectives, on_device(): lax.all_to_all(mixed, 'band', split_axis=0, concat_axis=0, tiled=True)  28.7 us
    pallas_call x1, Pallas kernels, filter_bands(): pl.pallas_call(functools.partial(filter_kernel, side, cells_x, cells_y),...  18.9 us
    all_gather x1, blocking collectives, on_device(): lax.all_gather(potential.reshape(1, rows, lanes), 'dom', axis=0, tiled=True)  15.6 us
    all_to_all x1, starting transfers between devices, on_device(): lax.all_to_all(panel, 'dom', split_axis=0, concat_axis=0, tiled=True)  4.22 us
    dot_general x1, matrix products, on_device(): lax.dot_general(full_ritz, block, (((0,), (0,)), ((), ())), preferred_ele...  2.86 us
    reshape x1, local copies, waits for them, and re-layouts, on_device(): panel = panel.reshape(rows, doms, share, lanes).transpose(1, 0, 2, 3)  2.61 us
  transfers between devices with their start and end apart: 2, of which 0 were waited for; matrix products, arithmetic and copies ran while one was open for 3% of the time, Pallas kernels for 15%

profile of v1, /device:TPU:0, one launch (start us, length us, event | category | flops | bytes accessed | tf_op | source)
XLA Modules:
  0.0 126.9 jit_solution(13717580015724246011)
XLA Ops:
  6.5 0.0 all-gather.2.cloned.1.call-start
  6.5 0.7 all-gather.2.cloned.1.call-update
  7.3 0.0 copy-start
  7.3 2.6 %copy.24 = bf16[32,4,32,128]{3,2,0,1:T(8,128)(2,1)} copy(bf16[32,4,32,128]{3,0,2,1:T(8,128)(2,1)} %bitcast.35) | data formatting | bytes 2097152 | tf_op jit(solution)/shard_map/reshape | solution.py:116
  9.9 4.2 %all-to-all-start = ((bf16[4,32,32,128]{3,2,1,0:T(8,128)(2,1)}), bf16[4,32,32,128]{3,2,1,0:T(8,128)(2,1)S(1)}, u32[]{:S(2)}, u32[]{:S(2)}) async-start(bf16[4,32,32,128]{3,2,1,0:T(8,128)(2,1)} %bitcast.28), calls=%async_computation | async-start | bytes 2097152 | tf_op jit(solution)/shard_map/all_to_all | solution.py:117
  14.1 0.0 copy-done
  14.1 15.6 %all_gather.6.pot_ref = f32[4,32,128]{2,1,0:T(8,128)S(1)} all-gather(f32[1,32,128]{2,1,0:T(8,128)S(1)} %bitcast.36), channel_id=1, replica_groups=mesh['dom'=4,'band'=8] {'dom'}, dimensions={0}, use_global_device_ids=true | all-gather | bytes 81920 | tf_op jit(solution)/shard_map/all_gather | solution.py:114
  29.7 0.0 all-to-all-done.in_ref
  29.7 18.9 %chebyshev.1 = bf16[4,32,32,128]{3,2,1,0:T(8,128)(2,1)S(1)} custom-call(bf16[4,32,32,128]{3,2,1,0:T(8,128)(2,1)S(1)} %all-to-all-done.in_ref, f32[4,32,128]{2,1,0:T(8,128)S(1)} %all_gather.6.pot_ref), custom_call_target="tpu_custom_call" | custom-call | tf_op jit(solution)/shard_map/chebyshev/pallas_call | solution.py:92
  48.7 0.1 copy.12
  48.8 36.4 %all_to_all.15 = bf16[32,4,32,128]{3,2,1,0:T(8,128)(2,1)S(1)} all-to-all(bf16[32,4,32,128]{3,2,1,0:T(8,128)(2,1)S(1)} %bitcast.31), channel_id=1, replica_groups=mesh['dom'=4,'band'=8] {'band','dom'}, dimensions={0} | all-to-all | bytes 2097152 | tf_op jit(solution)/shard_map/all_to_all | solution.py:122
  85.2 0.5 copy.13
  85.7 0.0 all-gather.2.cloned.1.call-done
  85.7 2.9 %fusion = bf16[64,8,8,128]{3,1,2,0:T(8,128)(2,1)S(1)} fusion(bf16[1024,1024]{1,0:T(8,128)(2,1)} %all-gather.2.cloned.1.call-done, bf16[128,8,4,128]{3,2,1,0:T(4,128)(2,1)S(1)} %bitcast.34), kind=kOutput, calls=%fused_computation.1 | convolution fusion | flops 1074266112 | bytes 4194304 | tf_op jit(solution)/shard_map/dot_general | solution.py:124
  88.6 0.3 copy.18
  88.9 0.2 copy.14
  89.1 28.7 %all_to_all.16 = bf16[8,128,4,128]{1,3,2,0:T(8,128)(2,1)S(1)} all-to-all(bf16[8,128,4,128]{1,3,2,0:T(8,128)(2,1)S(1)} %copy.14), channel_id=1, replica_groups=mesh['dom'=4,'band'=8] {'band'}, dimensions={0} | all-to-all | bytes 2097152 | tf_op jit(solution)/shard_map/all_to_all | solution.py:128
  117.8 0.2 convert_element_type.28
  118.1 2.0 %copy.15 = f32[128,1,2,16,128]{4,3,2,1,0:T(8,128)} copy(f32[128,1,2,16,128]{0,4,3,2,1:T(8,128)S(1)} %bitcast.30) | data formatting | bytes 4194304 | tf_op jit(solution)/shard_map/convert_element_type | solution.py:130
Async XLA Ops:
  6.5 79.2 %all-gather.2.cloned.1.call-start = ((), (), s32[]{:S(2)}) async-start(), calls=%async_computation.3 | async-start | bytes 2359296 | tf_op jit(solution)/shard_map/all_gather | solution.py:113
  7.3 6.8 %copy-start = (f32[1,2,16,128]{3,2,1,0:T(8,128)S(1)}, f32[1,2,16,128]{3,2,1,0:T(8,128)}, u32[]{:S(2)}) copy-start(f32[1,2,16,128]{3,2,1,0:T(8,128)} %param.4) | copy-start | bytes 49156
  9.9 19.9 %all-to-all-start = ((bf16[4,32,32,128]{3,2,1,0:T(8,128)(2,1)}), bf16[4,32,32,128]{3,2,1,0:T(8,128)(2,1)S(1)}, u32[]{:S(2)}, u32[]{:S(2)}) async-start(bf16[4,32,32,128]{3,2,1,0:T(8,128)(2,1)} %bitcast.28), calls=%async_computation | async-start | bytes 2097152 | tf_op jit(solution)/shard_map/all_to_all | solution.py:117
Sparse Core Ops, SparseCore 0:
  9.4 59.2 all-gather.1

commit v2 on v1

v2 whole, which is shorter than its diff:
```python
import functools
import math

import jax
import jax.numpy as jnp
from jax import lax
from jax.experimental import pallas as pl
from jax.experimental.pallas import tpu as pltpu
from jax.sharding import PartitionSpec as P

DEG = 4

lower_bound = -1.5
cut_off = 1.0
upper_bound = 9.5
coef_zero = -2.5
coef_one = 4.0 / 3.0
coef_two = -1.0 / 12.0


def filter_weights(degree):
    half_width = (upper_bound - cut_off) / 2.0
    centre = (upper_bound + cut_off) / 2.0
    sigma_now = half_width / (lower_bound - centre)
    first_scale = sigma_now / half_width
    inverse_gain = 2.0 / sigma_now
    weights = []
    for degree_step in range(1, degree):
        sigma_next = 1.0 / (inverse_gain - sigma_now)
        weights.append((2.0 * sigma_next / half_width, sigma_now * sigma_next))
        sigma_now = sigma_next
    return (centre, first_scale, weights)


def peer_of(index, doms):
    return {"band": lax.div(index, doms), "dom": lax.rem(index, doms)}


def loop(low, high, body, unroll=None):
    lax.fori_loop(low, high, lambda i, c: (body(i), c)[1], 0, unroll=unroll)


def filter_kernel(
    side, cells_x, cells_y, doms, groups,
    panel, pot_in, out_ref,
    pot_ref, got, done, even, odd,
    send_p, recv_p, here_p, send_a, recv_a, here_a, send_b, recv_b, here_b,
):
    chunks = panel.shape[0]
    count_x, count_y = even.shape[0], even.shape[1]
    part = out_ref.shape[2]
    total = doms * groups
    my_dom, my_group = lax.axis_index("dom"), lax.axis_index("band")
    me = my_group * doms + my_dom
    centre, first_scale, weights = filter_weights(DEG)
    diagonal = -0.5 * 3.0 * coef_zero - centre

    barrier = pltpu.get_barrier_semaphore()

    def greet(offset):
        pl.semaphore_signal(
            barrier, inc=1, device_id=peer_of(lax.rem(me + offset, total), doms),
            device_id_type=pl.DeviceIdType.MESH,
        )

    loop(1, total, greet)
    pl.semaphore_wait(barrier, total - 1)

    def copy_p(target, source):
        return pltpu.make_async_remote_copy(
            src_ref=pot_in,
            dst_ref=pot_ref.at[source],
            send_sem=send_p.at[target],
            recv_sem=recv_p.at[source],
            device_id={"dom": target},
            device_id_type=pl.DeviceIdType.MESH,
        )

    def copy_a(chunk, target, source):
        return pltpu.make_async_remote_copy(
            src_ref=panel.at[chunk, target],
            dst_ref=got.at[chunk, source],
            send_sem=send_a.at[chunk, target],
            recv_sem=recv_a.at[chunk, source],
            device_id={"dom": target},
            device_id_type=pl.DeviceIdType.MESH,
        )

    def copy_b(chunk, target, source):
        group, dom = lax.div(target, doms), lax.rem(target, doms)
        return pltpu.make_async_remote_copy(
            src_ref=done.at[chunk, dom, pl.ds(group * part, part)],
            dst_ref=out_ref.at[chunk, source],
            send_sem=send_b.at[chunk, target],
            recv_sem=recv_b.at[chunk, source],
            device_id=peer_of(target, doms),
            device_id_type=pl.DeviceIdType.MESH,
        )

    def local_a(chunk):
        return pltpu.make_async_copy(
            panel.at[chunk, my_dom], got.at[chunk, my_dom], here_a.at[chunk]
        )

    def local_b(chunk):
        return pltpu.make_async_copy(
            done.at[chunk, my_dom, pl.ds(my_group * part, part)],
            out_ref.at[chunk, me], here_b.at[chunk],
        )

    def other_dom(offset):
        return lax.rem(my_dom + offset, doms)

    def other(offset):
        return lax.rem(me + offset, total)

    def start_a(chunk):
        local_a(chunk).start()
        loop(1, doms, lambda o: copy_a(chunk, other_dom(o), my_dom).start())

    local_p = pltpu.make_async_copy(pot_in, pot_ref.at[my_dom], here_p)
    local_p.start()
    loop(1, doms, lambda o: copy_p(other_dom(o), my_dom).start())
    loop(0, chunks, start_a)
    local_p.wait()
    loop(1, doms, lambda o: copy_p(my_dom, other_dom(o)).wait_recv())

    def block_of(x, y):
        dom = (x // cells_x) * side + lax.div(y, cells_y)
        row = (x % cells_x) * cells_y + lax.rem(y, cells_y)
        return dom, row

    def load(chunk, y):
        for x in range(count_x):
            dom, row = block_of(x, y)
            even[x, y] = got[chunk, dom, row].astype(jnp.float32)

    def step(chunk, source, target, scale_h, scale_x, last):
        def row_step(y):
            at = lambda dy: lax.rem(y + dy + count_y, count_y)
            low, lower, high, higher = at(-1), at(-2), at(1), at(2)
            rows = [source[x, y] for x in range(count_x)]
            for x in range(count_x):
                here = rows[x]
                near = (
                    (rows[(x + 1) % count_x] + rows[(x - 1) % count_x])
                    + (source[x, low] + source[x, high])
                    + (pltpu.roll(here, 1, 1) + pltpu.roll(here, 127, 1))
                )
                far = (
                    (rows[(x + 2) % count_x] + rows[(x - 2) % count_x])
                    + (source[x, lower] + source[x, higher])
                    + (pltpu.roll(here, 2, 1) + pltpu.roll(here, 126, 1))
                )
                dom, row = block_of(x, y)
                pot = pot_ref[dom, pl.ds(row, 1), :] + diagonal
                value = (pot * scale_h) * here + (
                    (-0.5 * coef_one * scale_h) * near + (-0.5 * coef_two * scale_h) * far
                )
                if scale_x is not None:
                    value = value - scale_x * target[x, y]
                if last:
                    done[chunk, dom, row] = value.astype(done.dtype)
                else:
                    target[x, y] = value

        loop(0, count_y, row_step, unroll=2)

    def work(chunk):
        local_a(chunk).wait()
        loop(1, doms, lambda o: copy_a(chunk, my_dom, other_dom(o)).wait_recv())
        loop(0, count_y, lambda y: load(chunk, y), unroll=2)
        step(chunk, even, odd, first_scale, None, False)
        source, target = odd, even
        for index, (scale_h, scale_x) in enumerate(weights):
            step(chunk, source, target, scale_h, scale_x, index == len(weights) - 1)
            source, target = target, source
        loop(1, total, lambda o: copy_b(chunk, other(o), me).start())
        local_b(chunk).start()

    loop(0, chunks, work)

    loop(1, doms, lambda o: copy_p(other_dom(o), my_dom).wait_send())

    def finish(chunk):
        loop(1, doms, lambda o: copy_a(chunk, other_dom(o), my_dom).wait_send())
        local_b(chunk).wait()
        loop(1, total, lambda o: copy_b(chunk, other(o), me).wait_send())
        loop(1, total, lambda o: copy_b(chunk, other(o), other(o)).wait_recv())

    loop(0, chunks, finish)


def filter_bands(panel, potential, side, cells_x, cells_y, groups):
    chunks, doms, rows, bands, lanes = panel.shape
    total, part = doms * groups, rows // groups
    field = (side * cells_x, side * cells_y, bands, lanes)
    dma = pltpu.SemaphoreType.DMA
    return pl.pallas_call(
        functools.partial(filter_kernel, side, cells_x, cells_y, doms, groups),
        out_shape=jax.ShapeDtypeStruct((chunks, total, part, bands, lanes), jnp.bfloat16),
        in_specs=[pl.BlockSpec(memory_space=pltpu.VMEM)] * 2,
        out_specs=pl.BlockSpec(memory_space=pltpu.VMEM),
        scratch_shapes=[
            pltpu.VMEM((doms,) + potential.shape, jnp.float32),
            pltpu.VMEM(panel.shape, jnp.bfloat16),
            pltpu.VMEM(panel.shape, jnp.bfloat16),
            pltpu.VMEM(field, jnp.float32),
            pltpu.VMEM(field, jnp.float32),
            dma((doms,)),
            dma((doms,)),
            dma,
            dma((chunks, doms)),
            dma((chunks, doms)),
            dma((chunks,)),
            dma((chunks, total)),
            dma((chunks, total)),
            dma((chunks,)),
        ],
        compiler_params=pltpu.CompilerParams(
            vmem_limit_bytes=40 * 2**20, collective_id=0, has_side_effects=True
        ),
        name="chebyshev",
    )(panel, potential)


def on_device(orbitals, potential, ritz):
    doms = lax.axis_size("dom")
    groups = lax.axis_size("band")
    side = math.isqrt(doms)
    bands, _, cells_x, cells_y, lanes = orbitals.shape
    rows = cells_x * cells_y
    share = bands // doms
    deep = min(share, 16)
    chunks = share // deep
    part = rows // groups
    full_ritz = lax.all_gather(ritz, "band", axis=1, tiled=True)
    panel = orbitals.reshape(doms, chunks, deep, rows, lanes).transpose(1, 0, 3, 2, 4)
    block = filter_bands(panel, potential.reshape(rows, lanes), side, cells_x, cells_y, groups)
    block = block.reshape(chunks, groups * doms, part, deep, lanes).transpose(1, 0, 3, 2, 4)
    block = block.reshape(groups * bands, part * lanes)
    mixed = lax.dot_general(
        full_ritz, block, (((0,), (0,)), ((), ())), preferred_element_type=jnp.float32
    )
    mixed = mixed.astype(jnp.bfloat16).reshape(groups, bands, part, lanes)
    returned = lax.all_to_all(mixed, "band", split_axis=0, concat_axis=0, tiled=True)
    rotated = returned.transpose(1, 0, 2, 3).reshape(bands, rows, lanes)
    return rotated.astype(jnp.float32).reshape(orbitals.shape)


def solution(mesh):
    in_specs = (P("band", "dom", None, None, None), P("dom", None, None, None), P(None, "band"))
    out_specs = P("band", "dom", None, None, None)
    return jax.shard_map(
        on_device, mesh=mesh, in_specs=in_specs, out_specs=out_specs, check_vma=False
    )
```

time: 127 us -> 118 us (0.929)
  blocking collectives: 80.7 us -> 30.3 us
  Pallas kernels: 18.9 us -> 54.9 us
  waiting for transfers between devices: 0.73 us -> 11.6 us
  starting transfers between devices: 4.23 us -> 0.01 us
    all_to_all x1 -> x0, blocking collectives: 36.4 us -> none  [on_device(): lax.all_to_all(pieces, ('band', 'dom'), split_axis=0, concat_axis=0, tile...]
    pallas_call x1, Pallas kernels: 18.9 us -> 54.9 us  [filter_bands(): pl.pallas_call(functools.partial(filter_kernel, side, cells_x, cells_y, d...]
    all_gather x1 -> x0, blocking collectives: 15.6 us -> none  [on_device(): lax.all_gather(potential.reshape(1, rows, lanes), 'dom', axis=0, tiled=True)]
    all_gather x1, waiting for transfers between devices: 0.02 us -> 10.9 us  [on_device(): full_ritz = lax.all_gather(ritz, 'band', axis=1, tiled=True)]
    all_to_all x1 -> x0, starting transfers between devices: 4.22 us -> none  [on_device(): lax.all_to_all(panel, 'dom', split_axis=0, concat_axis=0, tiled=True)]
    all_to_all x1, blocking collectives: 28.7 us -> 30.3 us  [on_device(): lax.all_to_all(mixed, 'band', split_axis=0, concat_axis=0, tiled=True)]
    reshape x2 -> x1, local copies, waits for them, and re-layouts: 2.68 us -> 1.64 us  [on_device(): orbitals.reshape(doms, chunks, deep, rows, lanes).transpose(1, 0, 3, 2, 4)]
  transfers between devices with their start and end apart: 2 -> 1, of which waited for: 0 -> 1; matrix products, arithmetic and copies ran while one was open for 3% -> 2% of each run, Pallas kernels for 15% -> 47%
where the time goes in v2:
time: 118 us
  Pallas kernels  54.9 us (47%)
  blocking collectives  30.3 us (26%)
  between operations  13.4 us (11%)
  waiting for transfers between devices  11.6 us (10%)
  local copies, waits for them, and re-layouts  4.66 us (4%)
  matrix products  2.86 us (2%)
    pallas_call x1, Pallas kernels, filter_bands(): pl.pallas_call(functools.partial(filter_kernel, side, cells_x, cells_y, d...  54.9 us
    all_to_all x1, blocking collectives, on_device(): lax.all_to_all(mixed, 'band', split_axis=0, concat_axis=0, tiled=True)  30.3 us
    all_gather x1, waiting for transfers between devices, on_device(): full_ritz = lax.all_gather(ritz, 'band', axis=1, tiled=True)  10.9 us
    dot_general x1, matrix products, on_device(): lax.dot_general(full_ritz, block, (((0,), (0,)), ((), ())), preferred_ele...  2.86 us
  transfers between devices with their start and end apart: 1, of which 1 were waited for; matrix products, arithmetic and copies ran while one was open for 2% of the time, Pallas kernels for 47%

profile of v2, /device:TPU:0, one launch (start us, length us, event | category | flops | bytes accessed | tf_op | source)
XLA Modules:
  0.0 118.1 jit_solution(12399935487327254800)
XLA Ops:
  6.5 0.0 copy-start
  6.5 0.0 all-gather.2.cloned.1.call-start
  6.5 0.7 all-gather.2.cloned.1.call-update
  7.3 1.6 %copy.19 = bf16[4,2,16,32,128]{4,2,3,0,1:T(8,128)(2,1)S(1)} copy(bf16[4,2,16,32,128]{4,3,2,1,0:T(8,128)(2,1)} %bitcast.28) | data formatting | bytes 2097152 | tf_op jit(solution)/shard_map/reshape | solution.py:238
  8.9 0.0 copy-done
  8.9 54.9 %chebyshev.1 = bf16[2,32,4,16,128]{4,3,2,1,0:T(8,128)(2,1)S(1)} custom-call(bf16[2,4,32,16,128]{4,3,2,1,0:T(8,128)(2,1)S(1)} %bitcast.23, f32[32,128]{1,0:T(8,128)S(1)} %bitcast.24), custom_call_target="tpu_custom_call" | custom-call | tf_op jit(solution)/shard_map/chebyshev/pallas_call | solution.py:199
  63.9 0.5 copy.9
  64.4 10.9 %all-gather.2.cloned.1.call-done = bf16[1024,1024]{1,0:T(8,128)(2,1)} async-done(((bf16[1024,128]{1,0:T(8,128)(2,1)}), bf16[1024,1024]{1,0:T(8,128)(2,1)}) %all-gather.2.cloned.1.call-update) | async-done | bytes 2097168 | tf_op jit(solution)/shard_map/all_gather | solution.py:237
  75.3 2.9 %fusion = bf16[64,8,8,128]{3,1,2,0:T(8,128)(2,1)S(1)} fusion(bf16[1024,1024]{1,0:T(8,128)(2,1)} %all-gather.2.cloned.1.call-done, bf16[128,8,4,128]{3,2,1,0:T(4,128)(2,1)S(1)} %bitcast.27), kind=kOutput, calls=%fused_computation.1 | convolution fusion | flops 1074266112 | bytes 4194304 | tf_op jit(solution)/shard_map/dot_general | solution.py:242
  78.2 0.3 copy.13
  78.4 0.2 copy.10
  78.7 30.3 %all_to_all.5 = bf16[8,128,4,128]{1,3,2,0:T(8,128)(2,1)S(1)} all-to-all(bf16[8,128,4,128]{1,3,2,0:T(8,128)(2,1)S(1)} %copy.10), channel_id=1, replica_groups=mesh['dom'=4,'band'=8] {'band'}, dimensions={0} | all-to-all | bytes 2097152 | tf_op jit(solution)/shard_map/all_to_all | solution.py:246
  109.0 0.2 convert_element_type.28
  109.2 2.0 %copy.11 = f32[128,1,2,16,128]{4,3,2,1,0:T(8,128)} copy(f32[128,1,2,16,128]{0,4,3,2,1:T(8,128)S(1)} %bitcast.25) | data formatting | bytes 4194304 | tf_op jit(solution)/shard_map/convert_element_type | solution.py:248
Async XLA Ops:
  6.5 2.4 %copy-start = (f32[1,2,16,128]{3,2,1,0:T(8,128)S(1)}, f32[1,2,16,128]{3,2,1,0:T(8,128)}, u32[]{:S(2)}) copy-start(f32[1,2,16,128]{3,2,1,0:T(8,128)} %param.4) | copy-start | bytes 49156
  6.5 68.8 %all-gather.2.cloned.1.call-start = ((), (), s32[]{:S(2)}) async-start(), calls=%async_computation.1 | async-start | bytes 2359296 | tf_op jit(solution)/shard_map/all_gather | solution.py:237
Sparse Core Ops, SparseCore 0:
  9.4 65.8 all-gather.1

commit v3 on v2

--- a/solution.py
+++ b/solution.py
@@ -40,12 +40,19 @@
     lax.fori_loop(low, high, lambda i, c: (body(i), c)[1], 0, unroll=unroll)
 
 
-def filter_kernel(
-    side, cells_x, cells_y, doms, groups,
-    panel, pot_in, out_ref,
-    pot_ref, got, done, even, odd,
-    send_p, recv_p, here_p, send_a, recv_a, here_a, send_b, recv_b, here_b,
-):
+QUARTERS = 4
+
+
+def filter_kernel(side, cells_x, cells_y, doms, groups, fused, *refs):
+    if fused:
+        panel, pot_in, ritz_in, final = refs[:4]
+        out_ref, ritz_all, mixed, send_r, recv_r, here_r, send_x, recv_x, send_d, recv_d, here_d = refs[-11:]
+        refs = refs[4:-11]
+    else:
+        panel, pot_in, out_ref = refs[:3]
+        refs = refs[3:]
+    pot_ref, got, done, even, odd = refs[:5]
+    send_p, recv_p, here_p, send_a, recv_a, here_a, send_b, recv_b, here_b = refs[5:]
     chunks = panel.shape[0]
     count_x, count_y = even.shape[0], even.shape[1]
     part = out_ref.shape[2]
@@ -122,6 +129,44 @@
     local_p.start()
     loop(1, doms, lambda o: copy_p(other_dom(o), my_dom).start())
     loop(0, chunks, start_a)
+    if fused:
+        wide = ritz_in.shape[1]
+        quarter = lax.rem(my_dom, QUARTERS)
+        base = my_dom - quarter
+        across = lax.rem(quarter + 2, QUARTERS)
+        beside = quarter + 1 - 2 * lax.rem(quarter, 2)
+        opposite = lax.rem(beside + 2, QUARTERS)
+
+        def other_group(offset):
+            return lax.rem(my_group + offset, groups)
+
+        def copy_r(target, source):
+            return pltpu.make_async_remote_copy(
+                src_ref=ritz_in.at[quarter],
+                dst_ref=ritz_all.at[quarter, pl.ds(pl.multiple_of(source * wide, wide), wide)],
+                send_sem=send_r.at[target],
+                recv_sem=recv_r.at[source],
+                device_id={"band": target},
+                device_id_type=pl.DeviceIdType.MESH,
+            )
+
+        def copy_x(which, index, target):
+            return pltpu.make_async_remote_copy(
+                src_ref=ritz_all.at[index],
+                dst_ref=ritz_all.at[index],
+                send_sem=send_x.at[which],
+                recv_sem=recv_x.at[which],
+                device_id={"dom": base + target},
+                device_id_type=pl.DeviceIdType.MESH,
+            )
+
+        local_r = pltpu.make_async_copy(
+            ritz_in.at[quarter],
+            ritz_all.at[quarter, pl.ds(pl.multiple_of(my_group * wide, wide), wide)],
+            here_r,
+        )
+        local_r.start()
+        loop(1, groups, lambda o: copy_r(other_group(o), my_group).start())
     local_p.wait()
     loop(1, doms, lambda o: copy_p(my_dom, other_dom(o)).wait_recv())
 
@@ -178,7 +223,20 @@
         loop(1, total, lambda o: copy_b(chunk, other(o), me).start())
         local_b(chunk).start()
 
-    loop(0, chunks, work)
+    if fused:
+        loop(0, 1, work)
+        local_r.wait()
+        loop(1, groups, lambda o: copy_r(my_group, other_group(o)).wait_recv())
+        copy_x(0, quarter, across).start()
+        copy_x(1, quarter, beside).start()
+        loop(1, chunks, work)
+        copy_x(0, across, across).wait_recv()
+        copy_x(2, across, beside).start()
+        loop(1, groups, lambda o: copy_r(other_group(o), my_group).wait_send())
+        copy_x(1, beside, beside).wait_recv()
+        copy_x(2, opposite, beside).wait_recv()
+    else:
+        loop(0, chunks, work)
 
     loop(1, doms, lambda o: copy_p(other_dom(o), my_dom).wait_send())
 
@@ -189,39 +247,119 @@
         loop(1, total, lambda o: copy_b(chunk, other(o), other(o)).wait_recv())
 
     loop(0, chunks, finish)
-
-
-def filter_bands(panel, potential, side, cells_x, cells_y, groups):
+    if not fused:
+        return
+    copy_x(0, quarter, across).wait_send()
+    copy_x(1, quarter, beside).wait_send()
+    copy_x(2, across, beside).wait_send()
+
+    halves, pair = mixed.shape[0], mixed.shape[1]
+    deep, lanes = out_ref.shape[3], out_ref.shape[4]
+    depth = ritz_all.shape[2]
+    devices = depth // deep
+
+    def copy_d(half, target, source):
+        return pltpu.make_async_remote_copy(
+            src_ref=mixed.at[half, :, pl.ds(pl.multiple_of(target * wide, wide), wide)],
+            dst_ref=final.at[source, pl.ds(half * pair, pair)],
+            send_sem=send_d.at[half, target],
+            recv_sem=recv_d.at[half, source],
+            device_id={"band": target},
+            device_id_type=pl.DeviceIdType.MESH,
+        )
+
+    def local_d(half):
+        return pltpu.make_async_copy(
+            mixed.at[half, :, pl.ds(pl.multiple_of(my_group * wide, wide), wide)],
+            final.at[my_group, pl.ds(half * pair, pair)], here_d.at[half],
+        )
+
+    for half in range(halves):
+        columns = []
+        for q in range(QUARTERS):
+            chunk, first = (q * devices) // total, (q * devices) % total
+            pieces = [
+                out_ref[chunk, first : first + devices, half * pair + r].reshape(depth, lanes)
+                for r in range(pair)
+            ]
+            columns.append(jnp.concatenate(pieces, axis=1))
+
+        def rotate(g):
+            rows = pl.ds(pl.multiple_of(g * 256, 256), 256)
+            value = jnp.dot(ritz_all[0, rows, :], columns[0], preferred_element_type=jnp.float32)
+            for q in range(1, QUARTERS):
+                value = value + jnp.dot(
+                    ritz_all[q, rows, :], columns[q], preferred_element_type=jnp.float32
+                )
+            for r in range(pair):
+                mixed[half, r, rows, :] = value[:, r * lanes : (r + 1) * lanes].astype(mixed.dtype)
+
+        for g in range(ritz_all.shape[1] // 256):
+            rotate(g)
+        loop(1, groups, lambda o: copy_d(half, other_group(o), my_group).start())
+        local_d(half).start()
+
+    def receive(half):
+        local_d(half).wait()
+        loop(1, groups, lambda o: copy_d(half, other_group(o), my_group).wait_send())
+        loop(1, groups, lambda o: copy_d(half, other_group(o), other_group(o)).wait_recv())
+
+    loop(0, halves, receive)
+
+
+def filter_bands(panel, potential, ritz, side, cells_x, cells_y, groups):
     chunks, doms, rows, bands, lanes = panel.shape
     total, part = doms * groups, rows // groups
     field = (side * cells_x, side * cells_y, bands, lanes)
     dma = pltpu.SemaphoreType.DMA
+    blocks = (chunks, total, part, bands, lanes)
+    fused = ritz is not None
+    scratch = [
+        pltpu.VMEM((doms,) + potential.shape, jnp.float32),
+        pltpu.VMEM(panel.shape, jnp.bfloat16),
+        pltpu.VMEM(panel.shape, jnp.bfloat16),
+        pltpu.VMEM(field, jnp.float32),
+        pltpu.VMEM(field, jnp.float32),
+        dma((doms,)),
+        dma((doms,)),
+        dma,
+        dma((chunks, doms)),
+        dma((chunks, doms)),
+        dma((chunks,)),
+        dma((chunks, total)),
+        dma((chunks, total)),
+        dma((chunks,)),
+    ]
+    operands, result = (panel, potential), blocks
+    if fused:
+        _, wide, depth = ritz.shape
+        pair = 2 if part % 2 == 0 else 1
+        halves = part // pair
+        operands, result = (panel, potential, ritz), (groups, part, wide, lanes)
+        scratch += [
+            pltpu.VMEM(blocks, jnp.bfloat16),
+            pltpu.VMEM((QUARTERS, groups * wide, depth), jnp.bfloat16),
+            pltpu.VMEM((halves, pair, groups * wide, lanes), jnp.bfloat16),
+            dma((groups,)),
+            dma((groups,)),
+            dma,
+            dma((3,)),
+            dma((3,)),
+            dma((halves, groups)),
+            dma((halves, groups)),
+            dma((halves,)),
+        ]
     return pl.pallas_call(
-        functools.partial(filter_kernel, side, cells_x, cells_y, doms, groups),
-        out_shape=jax.ShapeDtypeStruct((chunks, total, part, bands, lanes), jnp.bfloat16),
-        in_specs=[pl.BlockSpec(memory_space=pltpu.VMEM)] * 2,
+        functools.partial(filter_kernel, side, cells_x, cells_y, doms, groups, fused),
+        out_shape=jax.ShapeDtypeStruct(result, jnp.bfloat16),
+        in_specs=[pl.BlockSpec(memory_space=pltpu.VMEM)] * len(operands),
         out_specs=pl.BlockSpec(memory_space=pltpu.VMEM),
-        scratch_shapes=[
-            pltpu.VMEM((doms,) + potential.shape, jnp.float32),
-            pltpu.VMEM(panel.shape, jnp.bfloat16),
-            pltpu.VMEM(panel.shape, jnp.bfloat16),
-            pltpu.VMEM(field, jnp.float32),
-            pltpu.VMEM(field, jnp.float32),
-            dma((doms,)),
-            dma((doms,)),
-            dma,
-            dma((chunks, doms)),
-            dma((chunks, doms)),
-            dma((chunks,)),
-            dma((chunks, total)),
-            dma((chunks, total)),
-            dma((chunks,)),
-        ],
+        scratch_shapes=scratch,
         compiler_params=pltpu.CompilerParams(
             vmem_limit_bytes=40 * 2**20, collective_id=0, has_side_effects=True
         ),
         name="chebyshev",
-    )(panel, potential)
+    )(*operands)
 
 
 def on_device(orbitals, potential, ritz):
@@ -234,9 +372,18 @@
     deep = min(share, 16)
     chunks = share // deep
     part = rows // groups
+    panel = orbitals.reshape(doms, chunks, deep, rows, lanes).transpose(1, 0, 3, 2, 4)
+    everyone = groups * bands
+    if deep == 16 and chunks == 2 and doms == QUARTERS and everyone % 1024 == 0 and bands % 16 == 0:
+        turned = ritz.reshape(groups, doms, chunks, deep, bands).transpose(4, 2, 0, 1, 3)
+        turned = turned.reshape(bands, QUARTERS, everyone // QUARTERS).transpose(1, 0, 2)
+        returned = filter_bands(
+            panel, potential.reshape(rows, lanes), turned, side, cells_x, cells_y, groups
+        )
+        rotated = returned.transpose(2, 0, 1, 3).reshape(bands, rows, lanes)
+        return rotated.astype(jnp.float32).reshape(orbitals.shape)
     full_ritz = lax.all_gather(ritz, "band", axis=1, tiled=True)
-    panel = orbitals.reshape(doms, chunks, deep, rows, lanes).transpose(1, 0, 3, 2, 4)
-    block = filter_bands(panel, potential.reshape(rows, lanes), side, cells_x, cells_y, groups)
+    block = filter_bands(panel, potential.reshape(rows, lanes), None, side, cells_x, cells_y, groups)
     block = block.reshape(chunks, groups * doms, part, deep, lanes).transpose(1, 0, 3, 2, 4)
     block = block.reshape(groups * bands, part * lanes)
     mixed = lax.dot_general(

time: 118 us -> 78.3 us (0.66)
  blocking collectives: 30.3 us -> 0 us
  Pallas kernels: 54.9 us -> 72.3 us
  between operations: 13.4 us -> 0.04 us
  waiting for transfers between devices: 11.6 us -> 0 us
  matrix products: 2.86 us -> 0 us
    all_to_all x1 -> x0, blocking collectives: 30.3 us -> none  [on_device(): lax.all_to_all(mixed, 'band', split_axis=0, concat_axis=0, tiled=True)]
    pallas_call x1, Pallas kernels: 54.9 us -> 72.3 us  [filter_bands(): pl.pallas_call(functools.partial(filter_kernel, side, cells_x, cells_y, d...]
    all_gather x1 -> x0, waiting for transfers between devices: 10.9 us -> none  [on_device(): full_ritz = lax.all_gather(ritz, 'band', axis=1, tiled=True)]
    dot_general x1 -> x0, matrix products: 2.86 us -> none  [on_device(): lax.dot_general(full_ritz, block, (((0,), (0,)), ((), ())), preferred_ele...]
  transfers between devices with their start and end apart: 1 -> 0, of which waited for: 1 -> 0; matrix products, arithmetic and copies ran while one was open for 2% -> 0% of each run, Pallas kernels for 47% -> 0%
where the time goes in v3:
time: 78.3 us; the launch traced here: 77.9 us
  Pallas kernels  72.3 us (92%)
  local copies, waits for them, and re-layouts  5.31 us (7%)
    pallas_call x1, Pallas kernels, filter_bands(): pl.pallas_call(functools.partial(filter_kernel, side, cells_x, cells_y, d...  72.3 us
    convert_element_type x1, local copies, waits for them, and re-layouts, on_device(): return rotated.astype(jnp.float32).reshape(orbitals.shape)  2.54 us
    reshape x1, local copies, waits for them, and re-layouts, on_device(): orbitals.reshape(doms, chunks, deep, rows, lanes).transpose(1, 0, 3, 2, 4)  1.64 us

profile of v3, /device:TPU:0, one launch (start us, length us, event | category | flops | bytes accessed | tf_op | source)
XLA Modules:
  0.0 77.9 jit_solution(16958222653354708985)
XLA Ops:
  0.0 0.0 copy-start
  0.0 1.0 %copy.9 = bf16[128,2,8,4,16]{0,4,3,2,1:T(8,128)(2,1)S(1)} copy(bf16[128,2,8,4,16]{0,4,1,3,2:T(8,128)(2,1)} %bitcast.19) | data formatting | bytes 524288 | tf_op jit(solution)/shard_map/transpose | solution.py:378
  1.0 0.1 copy.10
  1.1 1.6 %copy.13 = bf16[4,2,16,32,128]{4,2,3,0,1:T(8,128)(2,1)S(1)} copy(bf16[4,2,16,32,128]{4,3,2,1,0:T(8,128)(2,1)} %bitcast.17) | data formatting | bytes 2097152 | tf_op jit(solution)/shard_map/reshape | solution.py:375
  2.8 0.0 copy-done
  2.8 72.3 %chebyshev.1 = bf16[8,4,128,128]{3,2,1,0:T(8,128)(2,1)S(1)} custom-call(bf16[2,4,32,16,128]{4,3,2,1,0:T(8,128)(2,1)S(1)} %bitcast.13, f32[32,128]{1,0:T(8,128)S(1)} %bitcast.15, bf16[4,128,256]{2,1,0:T(8,128)(2,1)S(1)} %bitcast.14), custom_call_target="tpu_custom_call" | custom-call | tf_op jit(solution)/shard_map/chebyshev/pallas_call | solution.py:352
  75.1 0.2 convert_element_type.20
  75.4 2.5 %copy.11 = f32[128,1,2,16,128]{4,3,2,1,0:T(8,128)} copy(f32[128,1,2,16,128]{4,0,3,2,1:T(8,128)S(1)} %bitcast.16) | data formatting | bytes 4194304 | tf_op jit(solution)/shard_map/convert_element_type | solution.py:384
Async XLA Ops:
  0.0 2.8 %copy-start = (f32[1,2,16,128]{3,2,1,0:T(8,128)S(1)}, f32[1,2,16,128]{3,2,1,0:T(8,128)}, u32[]{:S(2)}) copy-start(f32[1,2,16,128]{3,2,1,0:T(8,128)} %param.4) | copy-start | bytes 49156

commit v4 on v3

--- a/solution.py
+++ b/solution.py
@@ -181,35 +181,53 @@
             even[x, y] = got[chunk, dom, row].astype(jnp.float32)
 
     def step(chunk, source, target, scale_h, scale_x, last):
-        def row_step(y):
-            at = lambda dy: lax.rem(y + dy + count_y, count_y)
-            low, lower, high, higher = at(-1), at(-2), at(1), at(2)
-            rows = [source[x, y] for x in range(count_x)]
+        tall = 4 if cells_y % 4 == 0 else 1
+        slab = min(8, even.shape[2])
+
+        def slab_step(first, bands):
+            ys = [lax.rem(first + (k - 2) + count_y, count_y) for k in range(tall + 4)]
+            rows = [[source[x, y, bands] for y in ys] for x in range(count_x)]
+            values = []
             for x in range(count_x):
-                here = rows[x]
-                near = (
-                    (rows[(x + 1) % count_x] + rows[(x - 1) % count_x])
-                    + (source[x, low] + source[x, high])
-                    + (pltpu.roll(here, 1, 1) + pltpu.roll(here, 127, 1))
-                )
-                far = (
-                    (rows[(x + 2) % count_x] + rows[(x - 2) % count_x])
-                    + (source[x, lower] + source[x, higher])
-                    + (pltpu.roll(here, 2, 1) + pltpu.roll(here, 126, 1))
-                )
+                dom, row = block_of(x, first)
+                for k in range(tall):
+                    here = rows[x][k + 2]
+                    side_near = rows[(x + 1) % count_x][k + 2] + rows[(x - 1) % count_x][k + 2]
+                    side_far = rows[(x + 2) % count_x][k + 2] + rows[(x - 2) % count_x][k + 2]
+                    near = (
+                        side_near
+                        + (rows[x][k + 1] + rows[x][k + 3])
+                        + (pltpu.roll(here, 1, 1) + pltpu.roll(here, 127, 1))
+                    )
+                    far = (
+                        side_far
+                        + (rows[x][k] + rows[x][k + 4])
+                        + (pltpu.roll(here, 2, 1) + pltpu.roll(here, 126, 1))
+                    )
+                    pot = (pot_ref[dom, pl.ds(row + k, 1), :] + diagonal) * scale_h
+                    value = pot * here + (
+                        (-0.5 * coef_one * scale_h) * near + (-0.5 * coef_two * scale_h) * far
+                    )
+                    if scale_x is not None:
+                        value = value - scale_x * target[x, first + k, bands]
+                    values.append((x, first + k, value))
+            for x, y, value in values:
+                target[x, y, bands] = value
+
+        def block_step(block):
+            for low in range(0, even.shape[2], slab):
+                slab_step(block * tall, pl.ds(low, slab))
+
+        loop(0, count_y // tall, block_step)
+        if not last:
+            return
+
+        def pack(y):
+            for x in range(count_x):
                 dom, row = block_of(x, y)
-                pot = pot_ref[dom, pl.ds(row, 1), :] + diagonal
-                value = (pot * scale_h) * here + (
-                    (-0.5 * coef_one * scale_h) * near + (-0.5 * coef_two * scale_h) * far
-                )
-                if scale_x is not None:
-                    value = value - scale_x * target[x, y]
-                if last:
-                    done[chunk, dom, row] = value.astype(done.dtype)
-                else:
-                    target[x, y] = value
-
-        loop(0, count_y, row_step, unroll=2)
+                done[chunk, dom, row] = target[x, y].astype(done.dtype)
+
+        loop(0, count_y, pack, unroll=4)
 
     def work(chunk):
         local_a(chunk).wait()

time: 78.3 us -> 76.1 us (0.972)
  Pallas kernels: 72.3 us -> 70.2 us
    pallas_call x1, Pallas kernels: 72.3 us -> 70.2 us  [filter_bands(): pl.pallas_call(functools.partial(filter_kernel, side, cells_x, cells_y, d...]
where the time goes in v4:
time: 76.1 us; the launch traced here: 75.8 us
  Pallas kernels  70.2 us (92%)
  local copies, waits for them, and re-layouts  5.31 us (7%)
    pallas_call x1, Pallas kernels, filter_bands(): pl.pallas_call(functools.partial(filter_kernel, side, cells_x, cells_y, d...  70.2 us
    convert_element_type x1, local copies, waits for them, and re-layouts, on_device(): return rotated.astype(jnp.float32).reshape(orbitals.shape)  2.54 us
    reshape x1, local copies, waits for them, and re-layouts, on_device(): orbitals.reshape(doms, chunks, deep, rows, lanes).transpose(1, 0, 3, 2, 4)  1.64 us

profile of v4, /device:TPU:0, one launch (start us, length us, event | category | flops | bytes accessed | tf_op | source)
XLA Modules:
  0.0 75.8 jit_solution(8588556577839427391)
XLA Ops:
  0.0 0.0 copy-start
  0.0 1.0 %copy.9 = bf16[128,2,8,4,16]{0,4,3,2,1:T(8,128)(2,1)S(1)} copy(bf16[128,2,8,4,16]{0,4,1,3,2:T(8,128)(2,1)} %bitcast.19) | data formatting | bytes 524288 | tf_op jit(solution)/shard_map/transpose | solution.py:396
  1.0 0.1 copy.10
  1.1 1.6 %copy.13 = bf16[4,2,16,32,128]{4,2,3,0,1:T(8,128)(2,1)S(1)} copy(bf16[4,2,16,32,128]{4,3,2,1,0:T(8,128)(2,1)} %bitcast.17) | data formatting | bytes 2097152 | tf_op jit(solution)/shard_map/reshape | solution.py:393
  2.8 0.0 copy-done
  2.8 70.2 %chebyshev.1 = bf16[8,4,128,128]{3,2,1,0:T(8,128)(2,1)S(1)} custom-call(bf16[2,4,32,16,128]{4,3,2,1,0:T(8,128)(2,1)S(1)} %bitcast.13, f32[32,128]{1,0:T(8,128)S(1)} %bitcast.15, bf16[4,128,256]{2,1,0:T(8,128)(2,1)S(1)} %bitcast.14), custom_call_target="tpu_custom_call" | custom-call | tf_op jit(solution)/shard_map/chebyshev/pallas_call | solution.py:370
  73.0 0.2 convert_element_type.20
  73.2 2.5 %copy.11 = f32[128,1,2,16,128]{4,3,2,1,0:T(8,128)} copy(f32[128,1,2,16,128]{4,0,3,2,1:T(8,128)S(1)} %bitcast.16) | data formatting | bytes 4194304 | tf_op jit(solution)/shard_map/convert_element_type | solution.py:402
Async XLA Ops:
  0.0 2.8 %copy-start = (f32[1,2,16,128]{3,2,1,0:T(8,128)S(1)}, f32[1,2,16,128]{3,2,1,0:T(8,128)}, u32[]{:S(2)}) copy-start(f32[1,2,16,128]{3,2,1,0:T(8,128)} %param.4) | copy-start | bytes 49156
